TPU v7x, 32 devices: a whole 2x2x4 slice. The times are simulated.
32 devices in a mesh: gx: 2 (over y), gy: 4 (over x, core), gz: 4 (over z).
Axes of the slice: x: 2, y: 2, z: 4, core: 2. Of those that a mesh axis runs over, the one named last changes fastest.
Arguments:
- right_side: float32 [32, 64, 256], P('gx', 'gy', 'gz'), may hold values from -8 to 8
- diagonal: float32 [32, 64, 256], P('gx', 'gy', 'gz'), may hold values from 0.001 to 0.01
Outputs:
- pressure: float32 [32, 64, 256], P('gx', 'gy', 'gz')
- residual: float32 [32, 64, 256], P('gx', 'gy', 'gz')
All inputs are finite; a program needn't handle non-finite values.
Results may differ from a plain program's by a relative error of at most 0.0003.
Values sent between devices are 32-bit elements; how exact they have to be, the bound alone decides.
A program may use at most 64 MiB of HBM per device.

v0:
```python
import jax
import jax.numpy as jnp
from jax import lax
from jax.sharding import PartitionSpec as P

DEGREE = 3


CHEB_LOW = 0.3
CHEB_HIGH = 2.0


def extended(block, sides, width):
    for axis, dim in sides:
        count = lax.axis_size(axis)
        forward = [(i, i + 1) for i in range(count - 1)]
        backward = [(target, source) for source, target in forward]
        low = lax.ppermute(
            lax.slice_in_dim(block, block.shape[dim] - width, None, axis=dim), axis, forward
        )
        high = lax.ppermute(lax.slice_in_dim(block, 0, width, axis=dim), axis, backward)
        block = jnp.concatenate([low, block, high], axis=dim)
    return block


def beside_sum(padded):
    neighbour_sum = padded[2:, 1:-1, 1:-1] + padded[:-2, 1:-1, 1:-1]
    neighbour_sum = neighbour_sum + padded[1:-1, 2:, 1:-1] + padded[1:-1, :-2, 1:-1]
    neighbour_sum = neighbour_sum + padded[1:-1, 1:-1, 2:] + padded[1:-1, 1:-1, :-2]
    return neighbour_sum


def restrict(values):
    first_len, second_len, third_len = values.shape
    blocks = values.reshape(first_len // 2, 2, second_len // 2, 2, third_len // 2, 2)
    return jnp.mean(blocks, axis=(1, 3, 5)) * 4.0


def prolong(values):
    first_len, second_len, third_len = values.shape
    widened = jnp.broadcast_to(
        values[:, None, :, None, :, None], (first_len, 2, second_len, 2, third_len, 2)
    )
    return widened.reshape(2 * first_len, 2 * second_len, 2 * third_len)


def chebyshev_constants():
    middle = 0.5 * (CHEB_HIGH + CHEB_LOW)
    spread_half = 0.5 * (CHEB_HIGH - CHEB_LOW)
    return (middle, spread_half, middle / spread_half)


def smooth(source, initial, added, operator, want_residual):
    inverse = 1.0 / (6.0 + added)
    middle, spread_half, sigma_one = chebyshev_constants()
    ratio_old = 1.0 / sigma_one
    if initial is None:
        residual = source
        update = inverse * residual / middle
        iterate = update
    else:
        residual = source - operator(initial, added)
        update = inverse * residual / middle
        iterate = initial + update
    for sweep in range(DEGREE - 1):
        residual = residual - operator(update, added)
        ratio_new = 1.0 / (2.0 * sigma_one - ratio_old)
        update = ratio_new * ratio_old * update + 2.0 * ratio_new / spread_half * inverse * residual
        iterate = iterate + update
        ratio_old = ratio_new
    if want_residual:
        residual = residual - operator(update, added)
    return (iterate, residual)


def fine_pad(values):
    return extended(values, (("gx", 0), ("gy", 1), ("gz", 2)), 1)


def fine_stencil(values, added):
    return (6.0 + added) * values - beside_sum(fine_pad(values))


def plain_stencil(values, added):
    return (6.0 + added) * values - beside_sum(jnp.pad(values, 1))


def coarse_cycle(source, added_three, added_four, operator):
    iterate, residual = smooth(source, None, added_three, operator, True)
    bottom, unused = smooth(restrict(residual), None, added_four, operator, False)
    iterate = iterate + prolong(bottom)
    iterate, unused = smooth(source, iterate, added_three, operator, False)
    return iterate


def assemble(rows, brick_shape, count_x, count_y, count_z):
    blocks = rows.reshape(count_x, count_y, count_z, brick_shape[0], brick_shape[1], brick_shape[2])
    blocks = blocks.transpose(0, 3, 1, 4, 2, 5)
    return blocks.reshape(
        count_x * brick_shape[0], count_y * brick_shape[1], count_z * brick_shape[2]
    )


def shards(right_side, diagonal):
    shifts = [diagonal]
    for tier_index in range(4):
        shifts.append(restrict(shifts[-1]))
    sources = [right_side]
    iterates = []
    for tier_index in range(3):
        iterate, residual = smooth(
            sources[tier_index], None, shifts[tier_index], fine_stencil, True
        )
        iterates.append(iterate)
        sources.append(restrict(residual))
    brick_shape = sources[3].shape
    count_x = lax.axis_size("gx")
    count_y = lax.axis_size("gy")
    count_z = lax.axis_size("gz")
    flat_source = sources[3].reshape(1, -1)
    flat_added = shifts[3].reshape(1, -1)
    all_source, all_added = (
        lax.all_gather(flat_source, ("gx", "gy", "gz"), axis=0, tiled=True),
        lax.all_gather(flat_added, ("gx", "gy", "gz"), axis=0, tiled=True),
    )
    whole_source = assemble(all_source, brick_shape, count_x, count_y, count_z)
    whole_added = assemble(all_added, brick_shape, count_x, count_y, count_z)
    whole_correction = coarse_cycle(whole_source, whole_added, restrict(whole_added), plain_stencil)
    starts = (
        lax.axis_index("gx") * brick_shape[0],
        lax.axis_index("gy") * brick_shape[1],
        lax.axis_index("gz") * brick_shape[2],
    )
    correction = lax.dynamic_slice(whole_correction, starts, brick_shape)
    for tier_index in (2, 1):
        iterate = iterates[tier_index] + prolong(correction)
        correction, unused = smooth(
            sources[tier_index], iterate, shifts[tier_index], fine_stencil, False
        )
    iterate = iterates[0] + prolong(correction)
    pressure, unused = smooth(right_side, iterate, diagonal, fine_stencil, False)
    return (pressure, right_side - fine_stencil(pressure, diagonal))


def solution(mesh):
    in_specs = (P("gx", "gy", "gz"), P("gx", "gy", "gz"))
    out_specs = (P("gx", "gy", "gz"), P("gx", "gy", "gz"))
    return jax.shard_map(shards, mesh=mesh, in_specs=in_specs, out_specs=out_specs, check_vma=False)
```

profile of v0, /device:TPU:0, one launch (start us, length us, event | category | flops | bytes accessed | tf_op | source)
XLA Modules:
  0.0 586.0 jit_solution(9958865523757006707)
XLA Ops:
  3.0 4.9 collective-permute-start.1
  15.9 5.2 collective-permute-start.5
  41.7 5.0 collective-permute-start.11
  66.4 5.0 collective-permute-start.17
  71.4 5.7 reshape.82
  79.9 5.7 reshape.83
  122.6 4.9 collective-permute-start.29
  160.7 5.0 collective-permute-start.39
  182.7 5.0 collective-permute-start.45
  194.4 71.0 %all-gather = f32[32,1,32]{2,1,0:T(1,128)S(1)} all-gather(f32[1,1,32]{2,1,0:T(1,128)S(1)} %reshape.94), channel_id=1, replica_groups=mesh['gx'=2,'gy'=4,'gz'=4] {'gx','gy','gz'}, dimensions={0}, use_global_device_ids=true | all-gather | bytes 4224 | tf_op jit(solution)/shard_map/all_gather | solution.py:124
  285.7 65.2 %all-gather.1 = f32[32,1,32]{2,1,0:T(1,128)S(1)} all-gather(f32[1,1,32]{2,1,0:T(1,128)S(1)} %reshape.96), channel_id=1, replica_groups=mesh['gx'=2,'gy'=4,'gz'=4] {'gx','gy','gz'}, dimensions={0}, use_global_device_ids=true | all-gather | bytes 4224 | tf_op jit(solution)/shard_map/all_gather | solution.py:123
  387.2 4.8 collective-permute-start.65
  395.0 4.7 collective-permute-start.67
  407.5 4.8 collective-permute-start.71
  444.2 5.0 collective-permute-start.81
  466.7 5.0 collective-permute-start.87
  483.4 4.9 reshape.93
  496.8 5.0 collective-permute-start.93
  521.0 5.1 collective-permute-start.99
  528.4 4.7 collective-permute-start.101
  545.3 5.1 collective-permute-start.105
  552.7 4.7 collective-permute-start.107
  569.6 5.1 collective-permute-start.111
  577.0 4.7 collective-permute-start.113
  (364 shorter events, 336.8 us)
Async XLA Ops:
  14.6 10.4 %collective-permute-start.4 = (f32[18,18,1]{2,1,0:T(8,128)S(1)}, f32[18,18,1]{2,1,0:T(8,128)S(1)}, u32[]{:S(2)}, u32[]{:S(2)}) collective-permute-start(f32[18,18,1]{2,1,0:T(8,128)S(1)} %get-tuple-element.48), channel_id=1, source_target_pairs={{1,0},{2,1},{3,2},{5,4},{6,5},{7,6},{9,8},{10,9},{11,10},{13,12},{... | collective-permute-start | bytes 3896 | tf_op jit(solution)/shard_map/ppermute | solution.py:21
  15.9 10.8 %collective-permute-start.5 = (f32[18,18,1]{2,1,0:T(8,128)S(1)}, f32[18,18,1]{2,1,0:T(8,128)S(1)}, u32[]{:S(2)}, u32[]{:S(2)}) collective-permute-start(f32[18,18,1]{2,1,0:T(8,128)S(1)} %get-tuple-element.49), channel_id=1, source_target_pairs={{0,1},{1,2},{2,3},{4,5},{5,6},{6,7},{8,9},{9,10},{10,11},{12,13},{... | collective-permute-start | bytes 3896 | tf_op jit(solution)/shard_map/ppermute | solution.py:18
  40.4 10.2 %collective-permute-start.10 = (f32[18,18,1]{2,1,0:T(8,128)S(1)}, f32[18,18,1]{2,1,0:T(8,128)S(1)}, u32[]{:S(2)}, u32[]{:S(2)}) collective-permute-start(f32[18,18,1]{2,1,0:T(8,128)S(1)} %get-tuple-element.46), channel_id=1, source_target_pairs={{1,0},{2,1},{3,2},{5,4},{6,5},{7,6},{9,8},{10,9},{11,10},{13,12},{... | collective-permute-start | bytes 3896 | tf_op jit(solution)/shard_map/ppermute | solution.py:21
  41.7 10.6 %collective-permute-start.11 = (f32[18,18,1]{2,1,0:T(8,128)S(1)}, f32[18,18,1]{2,1,0:T(8,128)S(1)}, u32[]{:S(2)}, u32[]{:S(2)}) collective-permute-start(f32[18,18,1]{2,1,0:T(8,128)S(1)} %get-tuple-element.47), channel_id=1, source_target_pairs={{0,1},{1,2},{2,3},{4,5},{5,6},{6,7},{8,9},{9,10},{10,11},{12,13},{... | collective-permute-start | bytes 3896 | tf_op jit(solution)/shard_map/ppermute | solution.py:18
  65.1 14.6 %collective-permute-start.16 = (f32[18,18,1]{2,1,0:T(8,128)S(1)}, f32[18,18,1]{2,1,0:T(8,128)S(1)}, u32[]{:S(2)}, u32[]{:S(2)}) collective-permute-start(f32[18,18,1]{2,1,0:T(8,128)S(1)} %get-tuple-element.44), channel_id=1, source_target_pairs={{1,0},{2,1},{3,2},{5,4},{6,5},{7,6},{9,8},{10,9},{11,10},{13,12},{... | collective-permute-start | bytes 3896 | tf_op jit(solution)/shard_map/ppermute | solution.py:21
  66.4 13.3 %collective-permute-start.17 = (f32[18,18,1]{2,1,0:T(8,128)S(1)}, f32[18,18,1]{2,1,0:T(8,128)S(1)}, u32[]{:S(2)}, u32[]{:S(2)}) collective-permute-start(f32[18,18,1]{2,1,0:T(8,128)S(1)} %get-tuple-element.45), channel_id=1, source_target_pairs={{0,1},{1,2},{2,3},{4,5},{5,6},{6,7},{8,9},{9,10},{10,11},{12,13},{... | collective-permute-start | bytes 3896 | tf_op jit(solution)/shard_map/ppermute | solution.py:18
  102.0 6.7 %collective-permute-start.23 = (f32[10,10,1]{2,1,0:T(8,128)S(1)}, f32[10,10,1]{2,1,0:T(8,128)S(1)}, u32[]{:S(2)}, u32[]{:S(2)}) collective-permute-start(f32[10,10,1]{2,1,0:T(8,128)S(1)} %get-tuple-element.89), channel_id=1, source_target_pairs={{0,1},{1,2},{2,3},{4,5},{5,6},{6,7},{8,9},{9,10},{10,11},{12,13},{... | collective-permute-start | bytes 1208 | tf_op jit(solution)/shard_map/ppermute | solution.py:18
  121.3 6.7 %collective-permute-start.28 = (f32[10,10,1]{2,1,0:T(8,128)S(1)}, f32[10,10,1]{2,1,0:T(8,128)S(1)}, u32[]{:S(2)}, u32[]{:S(2)}) collective-permute-start(f32[10,10,1]{2,1,0:T(8,128)S(1)} %get-tuple-element.86), channel_id=1, source_target_pairs={{1,0},{2,1},{3,2},{5,4},{6,5},{7,6},{9,8},{10,9},{11,10},{13,12},{... | collective-permute-start | bytes 1208 | tf_op jit(solution)/shard_map/ppermute | solution.py:21
  122.6 7.0 %collective-permute-start.29 = (f32[10,10,1]{2,1,0:T(8,128)S(1)}, f32[10,10,1]{2,1,0:T(8,128)S(1)}, u32[]{:S(2)}, u32[]{:S(2)}) collective-permute-start(f32[10,10,1]{2,1,0:T(8,128)S(1)} %get-tuple-element.87), channel_id=1, source_target_pairs={{0,1},{1,2},{2,3},{4,5},{5,6},{6,7},{8,9},{9,10},{10,11},{12,13},{... | collective-permute-start | bytes 1208 | tf_op jit(solution)/shard_map/ppermute | solution.py:18
  145.0 6.7 %collective-permute-start.35 = (f32[10,10,1]{2,1,0:T(8,128)S(1)}, f32[10,10,1]{2,1,0:T(8,128)S(1)}, u32[]{:S(2)}, u32[]{:S(2)}) collective-permute-start(f32[10,10,1]{2,1,0:T(8,128)S(1)} %get-tuple-element.85), channel_id=1, source_target_pairs={{0,1},{1,2},{2,3},{4,5},{5,6},{6,7},{8,9},{9,10},{10,11},{12,13},{... | collective-permute-start | bytes 1208 | tf_op jit(solution)/shard_map/ppermute | solution.py:18
  188.6 76.8 %collective-permute-start.46 = (f32[6,6,1]{2,1,0:T(8,128)S(1)}, f32[6,6,1]{2,1,0:T(8,128)S(1)}, u32[]{:S(2)}, u32[]{:S(2)}) collective-permute-start(f32[6,6,1]{2,1,0:T(8,128)S(1)} %get-tuple-element.126), channel_id=1, source_target_pairs={{1,0},{2,1},{3,2},{5,4},{6,5},{7,6},{9,8},{10,9},{11,10},{13,12},{... | collective-permute-start | bytes 440 | tf_op jit(solution)/shard_map/ppermute | solution.py:21
  189.9 75.5 %collective-permute-start.47 = (f32[6,6,1]{2,1,0:T(8,128)S(1)}, f32[6,6,1]{2,1,0:T(8,128)S(1)}, u32[]{:S(2)}, u32[]{:S(2)}) collective-permute-start(f32[6,6,1]{2,1,0:T(8,128)S(1)} %get-tuple-element.127), channel_id=1, source_target_pairs={{0,1},{1,2},{2,3},{4,5},{5,6},{6,7},{8,9},{9,10},{10,11},{12,13},{... | collective-permute-start | bytes 440 | tf_op jit(solution)/shard_map/ppermute | solution.py:18
  265.5 7.2 %collective-permute-start.48 = (f32[1,4,16]{2,1,0:T(4,128)S(1)}, f32[1,4,16]{2,1,0:T(4,128)S(1)}, u32[]{:S(2)}, u32[]{:S(2)}) collective-permute-start(f32[1,4,16]{2,1,0:T(4,128)S(1)} %get-tuple-element.152), channel_id=1, source_target_pairs={{16,0},{17,1},{18,2},{19,3},{20,4},{21,5},{22,6},{23,7},{24,8},{25... | collective-permute-start | bytes 776 | tf_op jit(solution)/shard_map/ppermute | solution.py:21
  429.0 6.6 %collective-permute-start.77 = (f32[10,10,1]{2,1,0:T(8,128)S(1)}, f32[10,10,1]{2,1,0:T(8,128)S(1)}, u32[]{:S(2)}, u32[]{:S(2)}) collective-permute-start(f32[10,10,1]{2,1,0:T(8,128)S(1)} %get-tuple-element.83), channel_id=1, source_target_pairs={{0,1},{1,2},{2,3},{4,5},{5,6},{6,7},{8,9},{9,10},{10,11},{12,13},{... | collective-permute-start | bytes 1208 | tf_op jit(solution)/shard_map/ppermute | solution.py:18
  451.4 6.7 %collective-permute-start.83 = (f32[10,10,1]{2,1,0:T(8,128)S(1)}, f32[10,10,1]{2,1,0:T(8,128)S(1)}, u32[]{:S(2)}, u32[]{:S(2)}) collective-permute-start(f32[10,10,1]{2,1,0:T(8,128)S(1)} %get-tuple-element.81), channel_id=1, source_target_pairs={{0,1},{1,2},{2,3},{4,5},{5,6},{6,7},{8,9},{9,10},{10,11},{12,13},{... | collective-permute-start | bytes 1208 | tf_op jit(solution)/shard_map/ppermute | solution.py:18
  474.0 6.7 %collective-permute-start.89 = (f32[10,10,1]{2,1,0:T(8,128)S(1)}, f32[10,10,1]{2,1,0:T(8,128)S(1)}, u32[]{:S(2)}, u32[]{:S(2)}) collective-permute-start(f32[10,10,1]{2,1,0:T(8,128)S(1)} %get-tuple-element.79), channel_id=1, source_target_pairs={{0,1},{1,2},{2,3},{4,5},{5,6},{6,7},{8,9},{9,10},{10,11},{12,13},{... | collective-permute-start | bytes 1208 | tf_op jit(solution)/shard_map/ppermute | solution.py:18
  502.9 7.9 %collective-permute-start.94 = (f32[18,18,1]{2,1,0:T(8,128)S(1)}, f32[18,18,1]{2,1,0:T(8,128)S(1)}, u32[]{:S(2)}, u32[]{:S(2)}) collective-permute-start(f32[18,18,1]{2,1,0:T(8,128)S(1)} %get-tuple-element.42), channel_id=1, source_target_pairs={{1,0},{2,1},{3,2},{5,4},{6,5},{7,6},{9,8},{10,9},{11,10},{13,12},{... | collective-permute-start | bytes 3896 | tf_op jit(solution)/shard_map/ppermute | solution.py:21
  504.2 8.1 %collective-permute-start.95 = (f32[18,18,1]{2,1,0:T(8,128)S(1)}, f32[18,18,1]{2,1,0:T(8,128)S(1)}, u32[]{:S(2)}, u32[]{:S(2)}) collective-permute-start(f32[18,18,1]{2,1,0:T(8,128)S(1)} %get-tuple-element.43), channel_id=1, source_target_pairs={{0,1},{1,2},{2,3},{4,5},{5,6},{6,7},{8,9},{9,10},{10,11},{12,13},{... | collective-permute-start | bytes 3896 | tf_op jit(solution)/shard_map/ppermute | solution.py:18
  527.1 8.0 %collective-permute-start.100 = (f32[18,18,1]{2,1,0:T(8,128)S(1)}, f32[18,18,1]{2,1,0:T(8,128)S(1)}, u32[]{:S(2)}, u32[]{:S(2)}) collective-permute-start(f32[18,18,1]{2,1,0:T(8,128)S(1)} %get-tuple-element.40), channel_id=1, source_target_pairs={{1,0},{2,1},{3,2},{5,4},{6,5},{7,6},{9,8},{10,9},{11,10},{13,12},{... | collective-permute-start | bytes 3896 | tf_op jit(solution)/shard_map/ppermute | solution.py:21
  528.4 8.2 %collective-permute-start.101 = (f32[18,18,1]{2,1,0:T(8,128)S(1)}, f32[18,18,1]{2,1,0:T(8,128)S(1)}, u32[]{:S(2)}, u32[]{:S(2)}) collective-permute-start(f32[18,18,1]{2,1,0:T(8,128)S(1)} %get-tuple-element.41), channel_id=1, source_target_pairs={{0,1},{1,2},{2,3},{4,5},{5,6},{6,7},{8,9},{9,10},{10,11},{12,13},{... | collective-permute-start | bytes 3896 | tf_op jit(solution)/shard_map/ppermute | solution.py:18
  551.4 8.0 %collective-permute-start.106 = (f32[18,18,1]{2,1,0:T(8,128)S(1)}, f32[18,18,1]{2,1,0:T(8,128)S(1)}, u32[]{:S(2)}, u32[]{:S(2)}) collective-permute-start(f32[18,18,1]{2,1,0:T(8,128)S(1)} %get-tuple-element.38), channel_id=1, source_target_pairs={{1,0},{2,1},{3,2},{5,4},{6,5},{7,6},{9,8},{10,9},{11,10},{13,12},{... | collective-permute-start | bytes 3896 | tf_op jit(solution)/shard_map/ppermute | solution.py:21
  552.7 8.2 %collective-permute-start.107 = (f32[18,18,1]{2,1,0:T(8,128)S(1)}, f32[18,18,1]{2,1,0:T(8,128)S(1)}, u32[]{:S(2)}, u32[]{:S(2)}) collective-permute-start(f32[18,18,1]{2,1,0:T(8,128)S(1)} %get-tuple-element.39), channel_id=1, source_target_pairs={{0,1},{1,2},{2,3},{4,5},{5,6},{6,7},{8,9},{9,10},{10,11},{12,13},{... | collective-permute-start | bytes 3896 | tf_op jit(solution)/shard_map/ppermute | solution.py:18
  575.7 8.0 %collective-permute-start.112 = (f32[18,18,1]{2,1,0:T(8,128)S(1)}, f32[18,18,1]{2,1,0:T(8,128)S(1)}, u32[]{:S(2)}, u32[]{:S(2)}) collective-permute-start(f32[18,18,1]{2,1,0:T(8,128)S(1)} %get-tuple-element.36), channel_id=1, source_target_pairs={{1,0},{2,1},{3,2},{5,4},{6,5},{7,6},{9,8},{10,9},{11,10},{13,12},{... | collective-permute-start | bytes 3896 | tf_op jit(solution)/shard_map/ppermute | solution.py:21
  577.0 8.2 %collective-permute-start.113 = (f32[18,18,1]{2,1,0:T(8,128)S(1)}, f32[18,18,1]{2,1,0:T(8,128)S(1)}, u32[]{:S(2)}, u32[]{:S(2)}) collective-permute-start(f32[18,18,1]{2,1,0:T(8,128)S(1)} %get-tuple-element.37), channel_id=1, source_target_pairs={{0,1},{1,2},{2,3},{4,5},{5,6},{6,7},{8,9},{9,10},{10,11},{12,13},{... | collective-permute-start | bytes 3896 | tf_op jit(solution)/shard_map/ppermute | solution.py:18
  (93 other events, 609.8 us)
where the time goes:
time: 595 us; the launch traced here: 586 us
  starting transfers between devices  327 us (55%)
  blocking collectives  136 us (23%)
  waiting for transfers between devices  82.3 us (14%)
  local copies, waits for them, and re-layouts  23.8 us (4%)
  other arithmetic  14.4 us (2%)
    ppermute x57, starting transfers between devices, extended(): lax.ppermute(lax.slice_in_dim(block, block.shape[dim] - width, None, axis...  253 us
    ppermute x57, starting transfers between devices, extended(): lax.ppermute(lax.slice_in_dim(block, 0, width, axis=dim), axis, backward)  73.6 us
    all_gather x1, blocking collectives, shards(): lax.all_gather(flat_added, ('gx', 'gy', 'gz'), axis=0, tiled=True)  71 us
    all_gather x1, blocking collectives, shards(): lax.all_gather(flat_source, ('gx', 'gy', 'gz'), axis=0, tiled=True)  65.2 us
    ppermute x57, waiting for transfers between devices, extended(): lax.ppermute(lax.slice_in_dim(block, block.shape[dim] - width, None, axis...  64.1 us
    ppermute x57, waiting for transfers between devices, extended(): lax.ppermute(lax.slice_in_dim(block, 0, width, axis=dim), axis, backward)  18.1 us
    reshape x5, local copies, waits for them, and re-layouts, restrict(): values.reshape(first_len // 2, 2, second_len // 2, 2, third_len // 2, 2)  12 us
  transfers between devices with their start and end apart: 114, of which 65 were waited for; matrix products, arithmetic and copies ran while one was open for 2% of the time, Pallas kernels for 0%

commit v1 on v0

v1 whole, which is shorter than its diff:
```python
import functools
import jax
import jax.numpy as jnp
from jax import lax
from jax.experimental import pallas as pl
from jax.experimental.pallas import tpu as pltpu
from jax.sharding import PartitionSpec as P

CHEB_LOW = 0.3
CHEB_HIGH = 2.0
MIDDLE = 0.5 * (CHEB_HIGH + CHEB_LOW)
HALF = 0.5 * (CHEB_HIGH - CHEB_LOW)
SIGMA = MIDDLE / HALF
Q0 = 1.0 / SIGMA
Q1 = 1.0 / (2.0 * SIGMA - Q0)
Q2 = 1.0 / (2.0 * SIGMA - Q1)
STEP0 = (0.0, 1.0 / MIDDLE)
STEP1 = (Q1 * Q0, 2.0 * Q1 / HALF)
STEP2 = (Q2 * Q1, 2.0 * Q2 / HALF)

MESH = pl.DeviceIdType.MESH
HX = 6
BF = jnp.bfloat16
F32 = jnp.float32


def ones_where(condition, value=1.0):
    return jnp.where(condition, value, 0.0).astype(BF)


def iota(shape, dim):
    return lax.broadcasted_iota(jnp.int32, shape, dim)


def split(values):
    high = values.astype(BF)
    return high, (values - high.astype(F32)).astype(BF)


def mm(values, matrix):
    high, low = split(values)
    return jnp.dot(high, matrix, preferred_element_type=F32) + jnp.dot(
        low, matrix, preferred_element_type=F32
    )


def mm_left(matrix, values):
    high, low = split(values)
    return jnp.dot(matrix, high, preferred_element_type=F32) + jnp.dot(
        matrix, low, preferred_element_type=F32
    )


class Level:
    def __init__(self, refs):
        self.r, self.diag, self.inv, self.v, self.d0, self.d1 = refs
        self.planes, self.rows, self.lanes = self.r.shape

    def loop(self, body, unroll):
        count = self.planes
        while count % unroll:
            unroll -= 1

        def step(k, carry):
            for u in range(unroll):
                body(k * unroll + u)
            return carry

        lax.fori_loop(0, count // unroll, step, 0)

    def clear(self):
        zeros = jnp.zeros(self.d0.shape[1:], F32)

        def step(x, carry):
            self.d0[x] = zeros
            self.d1[x] = zeros
            return carry

        lax.fori_loop(0, self.d0.shape[0], step, 0)

    def init(self, source, added, mask, plane_ok=None, unroll=2):
        def body(x):
            f = source(x)
            diag = 6.0 + added(x)
            inv = mask / diag
            if plane_ok is not None:
                inv = inv * plane_ok(x)
            d = inv * f * (1.0 / MIDDLE)
            self.r[x] = f
            self.diag[x] = diag
            self.inv[x] = inv
            self.v[x] = d
            self.d0[x + 1, 8 : 8 + self.rows] = d

        self.loop(body, unroll)

    def sweep(self, old, new, step, unroll=2, add_old=False):
        rows = self.rows

        def body(x):
            d = old[x + 1, 8 : 8 + rows]
            beside = old[x, 8 : 8 + rows] + old[x + 2, 8 : 8 + rows]
            beside = beside + old[x + 1, 7 : 7 + rows] + old[x + 1, 9 : 9 + rows]
            beside = beside + pltpu.roll(d, 1, 1) + pltpu.roll(d, self.lanes - 1, 1)
            r = self.r[x] - self.diag[x] * d + beside
            self.r[x] = r
            if step is None:
                return
            keep, gain = step
            fresh = gain * (self.inv[x] * r)
            if keep:
                fresh = keep * d + fresh
            new[x + 1, 8 : 8 + rows] = fresh
            self.v[x] = self.v[x] + (fresh + d if add_old else fresh)

        self.loop(body, unroll)

    def down(self, want_residual=True, unroll=2):
        self.sweep(self.d0, self.d1, STEP1, unroll)
        self.sweep(self.d1, self.d0, STEP2, unroll)
        if want_residual:
            self.sweep(self.d0, None, None, unroll)

    def up(self, want_residual=False, unroll=2):
        self.sweep(self.d0, self.d1, STEP0, unroll, add_old=True)
        self.sweep(self.d1, self.d0, STEP1, unroll)
        self.sweep(self.d0, self.d1, STEP2, unroll)
        if want_residual:
            self.sweep(self.d1, None, None, unroll)


def kernel(counts, f_ref, a_ref, p_ref, e_ref, turned, window, near_a, near_f, own_a, own_f,
           pack, gathered, whole_f, whole_a, f3, a3, f4, a4, *rest):
    gx, gy, gz = counts
    bx, by, bz = f_ref.shape
    devices = gx * gy * gz
    fine, mid, two, three, four = [Level(rest[6 * k : 6 * k + 6]) for k in range(5)]
    z_send, z_recv, w_send, w_recv, a_send, a_recv, f_send, f_recv, g_send, g_recv = rest[30:]
    me_x = lax.axis_index("gx")
    me_y = lax.axis_index("gy")
    me_z = lax.axis_index("gz")
    small_x = gx <= 2
    at_x = HX * me_x if small_x else HX
    at_one = (bx // 2) * me_x if small_x else bx // 2
    half_x, half_y, half_z = bx // 2, by // 2, bz // 2

    turned[...] = jnp.zeros_like(turned)
    padding = jnp.zeros((bx * by, 128 - bz), F32)
    for k, ref in enumerate((f_ref, a_ref)):
        flat = jnp.concatenate([ref[...].reshape(bx * by, bz), padding], axis=1)
        turned[0:bz, k * bx * by : (k + 1) * bx * by] = flat.T[0:bz]
    for ref in (near_a, near_f, whole_f, whole_a, f4, a4):
        ref[...] = jnp.zeros_like(ref)

    def clear_window(x, carry):
        window[0, x] = jnp.zeros(window.shape[2:], F32)
        window[1, x] = jnp.zeros(window.shape[2:], F32)
        return carry

    lax.fori_loop(0, window.shape[1], clear_window, 0)

    barrier = pltpu.get_barrier_semaphore()
    flat_me = (me_x * gy + me_y) * gz + me_z

    def place(k):
        other = lax.rem(flat_me + k, devices)
        return (lax.div(other, gy * gz), lax.rem(lax.div(other, gz), gy), lax.rem(other, gz))

    def greet(k, carry):
        pl.semaphore_signal(barrier, inc=1, device_id=place(k), device_id_type=MESH)
        return carry

    lax.fori_loop(1, devices, greet, 0)
    pl.semaphore_wait(barrier, devices - 1)

    def z_copy(way):
        src = turned.at[bz - 8 : bz] if way else turned.at[0:8]
        dst = turned.at[120:128] if way else turned.at[bz : bz + 8]
        return pltpu.make_async_remote_copy(
            src_ref=src, dst_ref=dst, send_sem=z_send.at[way], recv_sem=z_recv.at[way],
            device_id=(me_x, me_y, me_z + (1 if way else -1)), device_id_type=MESH)

    has_low, has_high = me_z > 0, me_z < gz - 1
    pl.when(has_high)(lambda: z_copy(1).start())
    pl.when(has_low)(lambda: z_copy(0).start())

    group = iota((4 * 128, 128), 0) // 128
    inner = iota((4 * 128, 128), 0) % 128
    column = iota((4 * 128, 128), 1)
    to_one = ones_where((column == group * 32 + inner // 2) & (inner < bz), 0.5)
    rows_one = ones_where(iota((half_y, by), 1) // 2 == iota((half_y, by), 0))

    def pack_one(plane, out):
        for q in range(half_x // 4):
            sums = jnp.concatenate(
                [plane(2 * (4 * q + j)) + plane(2 * (4 * q + j) + 1) for j in range(4)], axis=1)
            out[q] = mm_left(rows_one, mm(sums, to_one))

    pad_plane = jnp.zeros((by, 128 - bz), F32)
    pack_one(lambda x: jnp.concatenate([a_ref[x], pad_plane], axis=1), own_a)

    offsets_x = (0,) if gx == 1 else ((0, 2) if gx == 2 else (-1, 0, 1))

    def around():
        for ox in offsets_x:
            for oy in (-1, 0, 1):
                for oz in (-1, 0, 1):
                    if (ox, oy, oz) != (0, 0, 0):
                        yield ox, oy, oz

    def beside(ox, oy, oz):
        tx = me_x if ox == 0 else (1 - me_x if ox == 2 else me_x + ox)
        ty, tz = me_y + oy, me_z + oz
        there = None
        tests = []
        if abs(ox) == 1:
            tests.append((tx >= 0) & (tx < gx))
        if oy:
            tests.append(ty >= 0 if oy < 0 else ty < gy)
        if oz:
            tests.append(tz >= 0 if oz < 0 else tz < gz)
        for test in tests:
            there = test if there is None else there & test
        return (tx, ty, tz), there

    def guarded(there, act):
        if there is None:
            act()
        else:
            pl.when(there)(act)

    def brick_copy(offset, own, near, send, recv, arriving):
        ox, oy, oz = offset
        target, there = beside(ox, oy, oz)
        if arriving:
            slot_x = target[0] if small_x else 1 + ox
            slot = (slot_x * 3 + 1 + oy) * 3 + 1 + oz
        else:
            slot_x = me_x if small_x else 1 - ox
            slot = (slot_x * 3 + 1 - oy) * 3 + 1 - oz
        home = ((offsets_x.index(ox)) * 3 + 1 + oy) * 3 + 1 + oz
        copy = pltpu.make_async_remote_copy(
            src_ref=own, dst_ref=near.at[slot], send_sem=send.at[home], recv_sem=recv.at[slot],
            device_id=target, device_id_type=MESH)
        return copy, there

    def bricks(own, near, send, recv, what):
        for offset in around():
            copy, there = brick_copy(offset, own, near, send, recv, what == "recv")
            act = {"start": copy.start, "recv": copy.wait_recv, "send": copy.wait_send}[what]
            guarded(there, act)

    bricks(own_a, near_a, a_send, a_recv, "start")

    to_two = ones_where((column == group * 16 + inner // 2) & (inner < half_z), 0.5)
    to_two_a = ones_where((column == 64 + group * 16 + inner // 2) & (inner < half_z), 0.5)
    rows_two = ones_where(iota((half_y // 2, half_y), 1) // 2 == iota((half_y // 2, half_y), 0))
    lane = iota((8, 128), 1)

    def brick_plane(own, x):
        moved = own[x // 4]
        if x % 4:
            moved = pltpu.roll(moved, 128 - 32 * (x % 4), 1)
        return moved

    sums = jnp.concatenate(
        [brick_plane(own_a, 2 * i) + brick_plane(own_a, 2 * i + 1) for i in range(4)], axis=1)
    share_a = mm_left(rows_two, mm(sums, to_two_a))

    for level in (fine, mid, two, three, four):
        level.clear()
    pl.when(has_high)(lambda: z_copy(0).wait_recv())
    pl.when(has_low)(lambda: z_copy(1).wait_recv())
    for k in range(2):
        extended = turned[:, k * bx * by : (k + 1) * bx * by].T
        window[k, pl.ds(at_x, bx), 8 : 8 + by] = extended.reshape(bx, by, 128)

    def faces():
        for ox in offsets_x:
            for oy in (-1, 0, 1):
                if (ox, oy) != (0, 0):
                    yield ox, oy

    def face_copy(ox, oy, arriving):
        target, there = beside(ox, oy, 0)
        home = offsets_x.index(ox) * 3 + 1 + oy
        if ox == 0:
            src_x, dst_x, size_x = at_x, at_x, bx
        elif ox == 2:
            src_x = at_x + (bx - HX) * (1 - me_x)
            dst_x = bx * me_x
            size_x = HX
            if arriving:
                dst_x = bx * (1 - me_x)
        else:
            src_x = at_x + (bx - HX if ox == 1 else 0)
            dst_x = 0 if ox == 1 else HX + bx
            if arriving:
                dst_x = HX + bx if ox == 1 else 0
            size_x = HX
        src_y, size_y = {0: (8, by), 1: (by, 8), -1: (8, 8)}[oy]
        dst_y = {0: 8, 1: 0, -1: 8 + by}[-oy if arriving else oy]
        if arriving:
            recv = home
        else:
            recv = offsets_x.index(ox if ox in (0, 2) else -ox) * 3 + 1 - oy
        return pltpu.make_async_remote_copy(
            src_ref=window.at[:, pl.ds(src_x, size_x), src_y : src_y + size_y],
            dst_ref=window.at[:, pl.ds(dst_x, size_x), dst_y : dst_y + size_y],
            send_sem=w_send.at[home], recv_sem=w_recv.at[recv],
            device_id=target, device_id_type=MESH), there

    for ox, oy in faces():
        copy, there = face_copy(ox, oy, False)
        guarded(there, copy.start)

    zoff = iota((24, 128), 1)
    zoff = jnp.where(zoff < 96, zoff, zoff - 128)
    row = me_y * half_y - half_y + iota((24, 128), 0)
    z_at = me_z * half_z + zoff
    mask_one = jnp.where(
        (row >= 0) & (row < gy * half_y) & (z_at >= 0) & (z_at < gz * half_z) & (zoff < 64), 1.0, 0.0)
    lane_group = lane // 32

    def unpack_one(near, own, dst):
        near[(at_one // half_x) * 9 + 4] = own[...]
        for sx in range(min(gx, 3) if not small_x else gx):
            for sy in range(3):
                for q in range(half_x // 4):
                    base = (sx * 3 + sy) * 3
                    low = pltpu.roll(near[base, q], 96, 1)
                    mine = near[base + 1, q]
                    high = pltpu.roll(near[base + 2, q], 32, 1)
                    for j in range(4):
                        piece = jnp.where(
                            lane_group == j, mine,
                            jnp.where(lane_group == (j + 1) % 4, high,
                                      jnp.where(lane_group == (j + 3) % 4, low, 0.0)))
                        if j:
                            piece = pltpu.roll(piece, 128 - 32 * j, 1)
                        dst[sx * half_x + 4 * q + j, 8 * sy : 8 * sy + 8] = piece

    bricks(own_a, near_a, a_send, a_recv, "recv")
    unpack_one(near_a, own_a, mid.diag)

    zoff0 = iota((by + 16, 128), 1)
    zoff0 = jnp.where(zoff0 < 96, zoff0, zoff0 - 128)
    row0 = me_y * by - 8 + iota((by + 16, 128), 0)
    z0 = me_z * bz + zoff0
    mask_zero = jnp.where(
        (row0 >= 0) & (row0 < gy * by) & (z0 >= 0) & (z0 < gz * bz)
        & (zoff0 < bz + 8) & (zoff0 >= -8), 1.0, 0.0)

    def plane_ok(start, total):
        if small_x:
            return None
        return lambda x: jnp.where((start + x >= 0) & (start + x < total), 1.0, 0.0)

    for ox, oy in faces():
        copy, there = face_copy(ox, oy, True)
        guarded(there, copy.wait_recv)
    fine.init(lambda x: window[0, x], lambda x: window[1, x], mask_zero,
              plane_ok(me_x * bx - HX, gx * bx))
    fine.down()

    pack_one(lambda x: fine.r[at_x + x, 8 : 8 + by], own_f)
    bricks(own_f, near_f, f_send, f_recv, "start")
    bricks(own_f, near_f, f_send, f_recv, "recv")
    unpack_one(near_f, own_f, mid.r)
    mid.init(lambda x: mid.r[x], lambda x: mid.diag[x], mask_one,
             plane_ok(me_x * half_x - half_x, gx * half_x))
    mid.down()

    sums = jnp.concatenate(
        [mid.r[at_one + 2 * i, 8:16] + mid.r[at_one + 2 * i + 1, 8:16] for i in range(4)], axis=1)
    share = mm_left(rows_two, mm(sums, to_two)) + share_a
    pack[...] = share
    gathered[flat_me] = share

    def spread(k, carry):
        pltpu.make_async_remote_copy(
            src_ref=pack, dst_ref=gathered.at[flat_me], send_sem=g_send, recv_sem=g_recv,
            device_id=place(k), device_id_type=MESH).start()
        return carry

    lax.fori_loop(1, devices, spread, 0)
    everything = pltpu.make_async_remote_copy(
        src_ref=gathered.at[0 : devices - 1], dst_ref=gathered.at[0 : devices - 1],
        send_sem=g_send, recv_sem=g_recv, device_id=place(1), device_id_type=MESH)
    everything.wait_recv()

    lane16 = lane // 16

    def unpack_two(sx, carry):
        for pair in range(gy // 2):
            blocks = []
            for sz in range(gz):
                first = (sx * gy + 2 * pair) * gz + sz
                both = jnp.concatenate([gathered[first], gathered[first + gz]], axis=0)
                shift = 16 * (sz % 8)
                blocks.append(pltpu.roll(both, shift, 1) if shift else both)
            for k, dst in enumerate((whole_f, whole_a)):
                for i in range(4):
                    for tile in range((gz + 7) // 8):
                        piece = jnp.zeros((8, 128), F32)
                        for sz in range(8 * tile, min(gz, 8 * tile + 8)):
                            piece = jnp.where(lane16 == (4 * k + i + sz) % 8, blocks[sz], piece)
                        shift = (128 - 16 * (4 * k + i)) % 128
                        if shift:
                            piece = pltpu.roll(piece, shift, 1)
                        dst[4 * sx + i, 8 * pair : 8 * pair + 8, 128 * tile : 128 * tile + 128] = piece
        return carry

    lax.fori_loop(0, gx, unpack_two, 0)

    def whole_mask(level, rows, lanes):
        shape = (level.rows, level.lanes)
        return jnp.where((iota(shape, 0) < rows) & (iota(shape, 1) < lanes), 1.0, 0.0)

    def matrices(above, below):
        shape = (above.lanes, below.lanes)
        narrow = ones_where(iota(shape, 0) // 2 == iota(shape, 1), 0.5)
        shape = (below.rows, above.rows)
        return narrow, ones_where(iota(shape, 1) // 2 == iota(shape, 0))

    def restrict(src, dst, narrow, short):
        for i in range(dst.shape[0]):
            dst[i] = mm_left(short, mm(src[2 * i] + src[2 * i + 1], narrow))

    def prolong(values, dst, wide, tall):
        for i in range(values.shape[0]):
            spread_out = mm_left(tall, mm(values[i], wide))
            dst[2 * i + 1, 8 : 8 + dst.shape[1] - 16] = spread_out
            dst[2 * i + 2, 8 : 8 + dst.shape[1] - 16] = spread_out

    def wide_tall(above, below):
        shape = (below.lanes, above.lanes)
        wide = ones_where(iota(shape, 1) // 2 == iota(shape, 0))
        shape = (above.rows, below.rows)
        return wide, ones_where(iota(shape, 0) // 2 == iota(shape, 1))

    y2, z2 = gy * half_y // 2, gz * half_z // 2
    narrow2, short2 = matrices(two, three)
    narrow3, short3 = matrices(three, four)
    restrict(whole_a, a3, narrow2, short2)
    restrict(a3, a4, narrow3, short3)
    two.init(lambda x: whole_f[x], lambda x: whole_a[x], whole_mask(two, y2, z2), unroll=4)
    two.down(unroll=4)
    restrict(two.r, f3, narrow2, short2)
    three.init(lambda x: f3[x], lambda x: a3[x], whole_mask(three, y2 // 2, z2 // 2), unroll=4)
    three.down(unroll=4)
    restrict(three.r, f4, narrow3, short3)
    four.init(lambda x: f4[x], lambda x: a4[x], whole_mask(four, y2 // 4, z2 // 4))
    four.down(False)
    prolong(four.v, three.d0, *wide_tall(three, four))
    three.up(unroll=4)
    prolong(three.v, two.d0, *wide_tall(two, three))
    two.up(unroll=4)

    shape = (two.lanes, 128)
    zoff1 = iota(shape, 1)
    zoff1 = jnp.where(zoff1 < 96, zoff1, zoff1 - 128)
    coarse_z = (me_z * half_z + zoff1 + 2 * z2) // 2 - z2
    wide = ones_where((iota(shape, 0) == coarse_z) & (iota(shape, 0) < z2))
    shape = (mid.rows, two.rows)
    coarse_y = (me_y * half_y - half_y + iota(shape, 0) + 2 * y2) // 2 - y2
    tall = ones_where(iota(shape, 1) == coarse_y)
    pairs = mid.planes // 2
    for i in range(pairs):
        if small_x:
            values = two.v[i]
        else:
            at = me_x * (half_x // 2) - half_x // 2 + i
            inside = (at >= 0) & (at < two.planes)
            values = two.v[jnp.clip(at, 0, two.planes - 1)] * jnp.where(inside, 1.0, 0.0)
        spread_out = mm_left(tall, mm(values, wide))
        mid.d0[2 * i + 1, 8 : 8 + mid.rows] = spread_out
        mid.d0[2 * i + 2, 8 : 8 + mid.rows] = spread_out
    mid.up()

    shape = (128, 128)
    lane0 = iota(shape, 1)
    from_lane = jnp.where(lane0 < 96, lane0 // 2, 64 + lane0 // 2)
    wide = ones_where((iota(shape, 0) == from_lane) & ((lane0 < bz + 8) | (lane0 >= 120)))
    shape = (fine.rows, mid.rows)
    tall = ones_where(iota(shape, 1) == iota(shape, 0) // 2 + 4)
    at = (bx // 2 - HX // 2) * me_x if small_x else bx // 2 - HX // 2
    for i in range(fine.planes // 2):
        spread_out = mm_left(tall, mm(mid.v[at + i], wide))
        fine.d0[2 * i + 1, 8 : 8 + fine.rows] = spread_out
        fine.d0[2 * i + 2, 8 : 8 + fine.rows] = spread_out
    fine.up(True)
    p_ref[...] = fine.v[pl.ds(at_x, bx), 8 : 8 + by, 0:bz]
    e_ref[...] = fine.r[pl.ds(at_x, bx), 8 : 8 + by, 0:bz]

    pl.when(has_high)(lambda: z_copy(1).wait_send())
    pl.when(has_low)(lambda: z_copy(0).wait_send())
    bricks(own_a, near_a, a_send, a_recv, "send")
    bricks(own_f, near_f, f_send, f_recv, "send")
    for ox, oy in faces():
        copy, there = face_copy(ox, oy, False)
        guarded(there, copy.wait_send)
    everything.wait_send()


def shards(counts, right_side, diagonal):
    gx, gy, gz = counts
    bx, by, bz = right_side.shape
    slots_x = min(gx, 2) if gx <= 2 else 3
    x0 = bx + (HX * (gx - 1) if gx <= 2 else 2 * HX)

    def lanes_for(size):
        return 128 * ((size + 128) // 128)

    def level(planes, rows, lanes):
        plain = pltpu.VMEM((planes, rows, lanes), F32)
        padded = pltpu.VMEM((planes + 2, rows + 16, lanes), F32)
        return [plain] * 4 + [padded] * 2

    two = (gx * bx // 4, gy * by // 4, lanes_for(gz * bz // 4))
    three = (gx * bx // 8, gy * by // 8, lanes_for(gz * bz // 8))
    four = (gx * bx // 16, max(8, gy * by // 16), lanes_for(gz * bz // 16))
    brick = (bx // 8, by // 2, 128)
    near = (slots_x * 9,) + brick
    scratch = [
        pltpu.VMEM((128, 2 * bx * by), F32),
        pltpu.VMEM((2, x0, by + 16, 128), F32),
        pltpu.VMEM(near, F32),
        pltpu.VMEM(near, F32),
        pltpu.VMEM(brick, F32),
        pltpu.VMEM(brick, F32),
        pltpu.VMEM((by // 4, 128), F32),
        pltpu.VMEM((gx * gy * gz, by // 4, 128), F32),
        pltpu.VMEM(two, F32),
        pltpu.VMEM(two, F32),
        pltpu.VMEM(three, F32),
        pltpu.VMEM(three, F32),
        pltpu.VMEM(four, F32),
        pltpu.VMEM(four, F32),
    ]
    scratch += level(x0, by + 16, 128)
    scratch += level(slots_x * bx // 2, 24, 128)
    scratch += level(*two) + level(*three) + level(*four)
    dma = pltpu.SemaphoreType.DMA
    scratch += [dma((2,)), dma((2,))]
    scratch += [dma((slots_x * 3,))] * 2
    scratch += [dma((slots_x * 9,))] * 4
    scratch += [dma, dma]
    out = jax.ShapeDtypeStruct(right_side.shape, F32)
    vmem = pl.BlockSpec(memory_space=pltpu.VMEM)
    return pl.pallas_call(
        functools.partial(kernel, counts),
        out_shape=(out, out),
        in_specs=[vmem, vmem],
        out_specs=(vmem, vmem),
        scratch_shapes=scratch,
        compiler_params=pltpu.CompilerParams(
            collective_id=0, has_side_effects=True, vmem_limit_bytes=56 * 1024 * 1024
        ),
    )(right_side, diagonal)


def solution(mesh):
    spec = P("gx", "gy", "gz")
    counts = tuple(mesh.shape[name] for name in ("gx", "gy", "gz"))
    return jax.shard_map(
        functools.partial(shards, counts), mesh=mesh, in_specs=(spec, spec),
        out_specs=(spec, spec), check_vma=False)
```

time: 595 us -> 48.7 us (0.08); the launches traced: 586 us -> 48.6 us
  starting transfers between devices: 327 us -> 0 us
  blocking collectives: 136 us -> 0 us
  waiting for transfers between devices: 82.3 us -> 0 us
  Pallas kernels: 0 us -> 45.7 us
  local copies, waits for them, and re-layouts: 23.8 us -> 2.26 us
  other arithmetic: 14.4 us -> 0 us
    ppermute x114 -> x0, starting transfers between devices: 327 us -> none  [the longest x57 253 us: extended(): lax.ppermute(lax.slice_in_dim(block, block.shape[dim] - width, None, axis...]
    all_gather x2 -> x0, blocking collectives: 136 us -> none  [the longest x1 71 us: shards(): lax.all_gather(flat_added, ('gx', 'gy', 'gz'), axis=0, tiled=True)]
    ppermute x114 -> x0, waiting for transfers between devices: 82.3 us -> none  [the longest x57 64.1 us: extended(): lax.ppermute(lax.slice_in_dim(block, block.shape[dim] - width, None, axis...]
    pallas_call x0 -> x1, Pallas kernels: none -> 45.7 us  [shards(): pl.pallas_call(functools.partial(kernel, counts), out_shape=(out, out), i...]
    reshape x13 -> x0, local copies, waits for them, and re-layouts: 17.7 us -> none  [the longest x5 12 us: restrict(): values.reshape(first_len // 2, 2, second_len // 2, 2, third_len // 2, 2)]
  transfers between devices with their start and end apart: 114 -> 0, of which waited for: 65 -> 0; matrix products, arithmetic and copies ran while one was open for 2% -> 0% of each run, Pallas kernels for 0% -> 0%
where the time goes in v1:
time: 48.7 us; the launch traced here: 48.6 us
  Pallas kernels  45.7 us (94%)
  local copies, waits for them, and re-layouts  2.26 us (5%)
  between operations  0.65 us (1%)
    pallas_call x1, Pallas kernels, shards(): pl.pallas_call(functools.partial(kernel, counts), out_shape=(out, out), i...  45.7 us
    unnamed x4, local copies, waits for them, and re-layouts  2.26 us

profile of v1, /device:TPU:0, one launch (start us, length us, event | category | flops | bytes accessed | tf_op | source)
XLA Modules:
  0.0 48.6 jit_solution(13169432881888867012)
XLA Ops:
  0.6 45.7 %shard_map.41 = (f32[16,16,64]{2,1,0:T(8,128)}, f32[16,16,64]{2,1,0:T(8,128)}) custom-call(f32[16,16,64]{2,1,0:T(8,128)} %f_ref.1, f32[16,16,64]{2,1,0:T(8,128)} %a_ref.1), custom_call_target="tpu_custom_call" | custom-call | tf_op jit(solution)/shard_map/pallas_call | solution.py:551
  46.3 0.0 copy-start
  46.3 1.6 %copy.6 = f32[16,16,64]{2,1,0:T(8,128)} copy(f32[16,16,64]{2,1,0:T(8,128)} %get-tuple-element.4) | data formatting | bytes 131072
  47.9 0.0 copy-done
  47.9 0.7 %copy.7 = f32[16,16,64]{2,1,0:T(8,128)} copy(f32[16,16,64]{2,1,0:T(8,128)S(1)} %copy-done) | data formatting | bytes 131072
Async XLA Ops:
  46.3 1.6 %copy-start = (f32[16,16,64]{2,1,0:T(8,128)S(1)}, f32[16,16,64]{2,1,0:T(8,128)}, u32[]{:S(2)}) copy-start(f32[16,16,64]{2,1,0:T(8,128)} %get-tuple-element.5) | copy-start | bytes 196612

commit v2 on v1

--- a/solution.py
+++ b/solution.py
@@ -32,101 +32,138 @@
     return lax.broadcasted_iota(jnp.int32, shape, dim)
 
 
-def split(values):
-    high = values.astype(BF)
-    return high, (values - high.astype(F32)).astype(BF)
-
-
 def mm(values, matrix):
-    high, low = split(values)
-    return jnp.dot(high, matrix, preferred_element_type=F32) + jnp.dot(
-        low, matrix, preferred_element_type=F32
-    )
+    rows = values.shape[0]
+    high = values.astype(BF).astype(F32)
+    both = jnp.concatenate([high, values - high], axis=0).astype(BF)
+    out = jnp.dot(both, matrix, preferred_element_type=F32)
+    return out[:rows] + out[rows:]
 
 
 def mm_left(matrix, values):
-    high, low = split(values)
-    return jnp.dot(matrix, high, preferred_element_type=F32) + jnp.dot(
-        matrix, low, preferred_element_type=F32
-    )
+    lanes = values.shape[1]
+    high = values.astype(BF).astype(F32)
+    both = jnp.concatenate([high, values - high], axis=1).astype(BF)
+    out = jnp.dot(matrix, both, preferred_element_type=F32)
+    return out[:, :lanes] + out[:, lanes:]
 
 
 class Level:
-    def __init__(self, refs):
-        self.r, self.diag, self.inv, self.v, self.d0, self.d1 = refs
+    def __init__(self, refs, halo=0, sides=0, me=0):
+        self.r, self.diag, self.inv, self.v, self.d0, self.d1, self.d2 = refs
         self.planes, self.rows, self.lanes = self.r.shape
-
-    def loop(self, body, unroll):
-        count = self.planes
-        while count % unroll:
-            unroll -= 1
+        self.halo, self.sides, self.me = halo, sides, me
+        self.group = max(1, 8 // (self.rows // 8 * (self.lanes // 128)))
+
+    def loop(self, body, halo=0):
+        trim = self.halo - halo
+        count = self.planes - self.sides * trim
+        base = {0: 0, 1: trim * self.me, 2: trim}[self.sides]
+        if count <= 32:
+            at = 0
+            while at < count:
+                size = min(self.group, count - at)
+                body(base + at, size)
+                at += size
+            return
+        size = next(k for k in (4, 3, 2, 1) if count % k == 0)
 
         def step(k, carry):
-            for u in range(unroll):
-                body(k * unroll + u)
+            body(base + k * size, size)
             return carry
 
-        lax.fori_loop(0, count // unroll, step, 0)
+        lax.fori_loop(0, count // size, step, 0)
 
     def clear(self):
         zeros = jnp.zeros(self.d0.shape[1:], F32)
-
-        def step(x, carry):
-            self.d0[x] = zeros
-            self.d1[x] = zeros
-            return carry
-
-        lax.fori_loop(0, self.d0.shape[0], step, 0)
-
-    def init(self, source, added, mask, plane_ok=None, unroll=2):
-        def body(x):
-            f = source(x)
-            diag = 6.0 + added(x)
-            inv = mask / diag
-            if plane_ok is not None:
-                inv = inv * plane_ok(x)
-            d = inv * f * (1.0 / MIDDLE)
-            self.r[x] = f
-            self.diag[x] = diag
-            self.inv[x] = inv
-            self.v[x] = d
-            self.d0[x + 1, 8 : 8 + self.rows] = d
-
-        self.loop(body, unroll)
-
-    def sweep(self, old, new, step, unroll=2, add_old=False):
+        edge = jnp.zeros(self.d0.shape[:1] + (8,) + self.d0.shape[2:], F32)
+        for d in (self.d0, self.d1, self.d2):
+            d[0] = zeros
+            d[self.planes + 1] = zeros
+            d[:, 0:8] = edge
+            d[:, 8 + self.rows :] = edge
+
+    def scale(self, added, mask, plane_ok=None):
+        def body(x0, size):
+            for x in range(size):
+                diag = 6.0 + added(x0 + x)
+                inv = mask / diag
+                if plane_ok is not None:
+                    inv = inv * plane_ok(x0 + x)
+                self.diag[x0 + x] = diag
+                self.inv[x0 + x] = inv
+
+        self.loop(body, self.halo)
+
+    def init(self, source):
         rows = self.rows
 
-        def body(x):
-            d = old[x + 1, 8 : 8 + rows]
-            beside = old[x, 8 : 8 + rows] + old[x + 2, 8 : 8 + rows]
-            beside = beside + old[x + 1, 7 : 7 + rows] + old[x + 1, 9 : 9 + rows]
-            beside = beside + pltpu.roll(d, 1, 1) + pltpu.roll(d, self.lanes - 1, 1)
-            r = self.r[x] - self.diag[x] * d + beside
-            self.r[x] = r
-            if step is None:
-                return
-            keep, gain = step
-            fresh = gain * (self.inv[x] * r)
-            if keep:
-                fresh = keep * d + fresh
-            new[x + 1, 8 : 8 + rows] = fresh
-            self.v[x] = self.v[x] + (fresh + d if add_old else fresh)
-
-        self.loop(body, unroll)
-
-    def down(self, want_residual=True, unroll=2):
-        self.sweep(self.d0, self.d1, STEP1, unroll)
-        self.sweep(self.d1, self.d0, STEP2, unroll)
+        def body(x0, size):
+            f = [source(x0 + x) for x in range(size)]
+            d = [self.inv[x0 + x] * f[x] * (1.0 / MIDDLE) for x in range(size)]
+            for x in range(size):
+                self.r[x0 + x] = f[x]
+                self.d0[x0 + x + 1, 8 : 8 + rows] = d[x]
+
+        self.loop(body, self.halo)
+
+    def sweep(self, old, new, step, halo):
+        rows = self.rows
+
+        def body(x0, size):
+            ds = [old[x0 + k, 8 : 8 + rows] for k in range(size + 2)]
+            rs, fresh = [], []
+            for k in range(size):
+                d = ds[k + 1]
+                beside = ds[k] + ds[k + 2]
+                beside = beside + (old[x0 + k + 1, 7 : 7 + rows] + old[x0 + k + 1, 9 : 9 + rows])
+                beside = beside + (pltpu.roll(d, 1, 1) + pltpu.roll(d, self.lanes - 1, 1))
+                r = self.r[x0 + k] - self.diag[x0 + k] * d + beside
+                rs.append(r)
+                if step is not None:
+                    keep, gain = step
+                    e = gain * (self.inv[x0 + k] * r)
+                    fresh.append(keep * d + e if keep else e)
+            for k in range(size):
+                self.r[x0 + k] = rs[k]
+                if step is not None:
+                    new[x0 + k + 1, 8 : 8 + rows] = fresh[k]
+
+        self.loop(body, halo)
+
+    def total(self, halo, first):
+        rows = self.rows
+
+        def body(x0, size):
+            for k in range(size):
+                at = (x0 + k + 1, slice(8, 8 + rows))
+                sums = self.d0[at] + self.d1[at] + self.d2[at]
+                self.v[x0 + k] = sums if first else self.v[x0 + k] + sums
+
+        self.loop(body, halo)
+
+    def total_last(self, halo=0):
+        def body(x0, size):
+            for k in range(size):
+                self.v[x0 + k] = self.v[x0 + k] + self.d0[x0 + k + 1, 8 : 8 + self.rows]
+
+        self.loop(body, halo)
+
+    def down(self, halo=0, want_residual=True):
+        step = 1 if self.sides else 0
+        self.sweep(self.d0, self.d1, STEP1, halo + 2 * step)
+        self.sweep(self.d1, self.d2, STEP2, halo + step)
         if want_residual:
-            self.sweep(self.d0, None, None, unroll)
-
-    def up(self, want_residual=False, unroll=2):
-        self.sweep(self.d0, self.d1, STEP0, unroll, add_old=True)
-        self.sweep(self.d1, self.d0, STEP1, unroll)
-        self.sweep(self.d0, self.d1, STEP2, unroll)
+            self.sweep(self.d2, None, None, halo)
+
+    def up(self, halo=0, want_residual=False):
+        step = 1 if self.sides else 0
+        self.sweep(self.d0, self.d1, STEP0, halo + 2 * step)
+        self.sweep(self.d1, self.d2, STEP1, halo + step)
+        self.total(halo, False)
+        self.sweep(self.d2, self.d0, STEP2, halo)
         if want_residual:
-            self.sweep(self.d1, None, None, unroll)
+            self.sweep(self.d0, None, None, halo - step)
 
 
 def kernel(counts, f_ref, a_ref, p_ref, e_ref, turned, window, near_a, near_f, own_a, own_f,
@@ -134,12 +171,15 @@
     gx, gy, gz = counts
     bx, by, bz = f_ref.shape
     devices = gx * gy * gz
-    fine, mid, two, three, four = [Level(rest[6 * k : 6 * k + 6]) for k in range(5)]
-    z_send, z_recv, w_send, w_recv, a_send, a_recv, f_send, f_recv, g_send, g_recv = rest[30:]
+    z_send, z_recv, w_send, w_recv, a_send, a_recv, f_send, f_recv, g_send, g_recv = rest[35:]
     me_x = lax.axis_index("gx")
     me_y = lax.axis_index("gy")
     me_z = lax.axis_index("gz")
     small_x = gx <= 2
+    sides = gx - 1 if small_x else 2
+    fine = Level(rest[0:7], HX, sides, me_x)
+    mid = Level(rest[7:14], bx // 2, sides, me_x)
+    two, three, four = [Level(rest[7 * k : 7 * k + 7]) for k in (2, 3, 4)]
     at_x = HX * me_x if small_x else HX
     at_one = (bx // 2) * me_x if small_x else bx // 2
     half_x, half_y, half_z = bx // 2, by // 2, bz // 2
@@ -184,20 +224,37 @@
     pl.when(has_high)(lambda: z_copy(1).start())
     pl.when(has_low)(lambda: z_copy(0).start())
 
-    group = iota((4 * 128, 128), 0) // 128
-    inner = iota((4 * 128, 128), 0) % 128
-    column = iota((4 * 128, 128), 1)
-    to_one = ones_where((column == group * 32 + inner // 2) & (inner < bz), 0.5)
-    rows_one = ones_where(iota((half_y, by), 1) // 2 == iota((half_y, by), 0))
-
-    def pack_one(plane, out):
+    inner = iota((128, 128), 0)
+    column = iota((128, 128), 1)
+
+    def packing(width, kept, start):
+        return jnp.concatenate(
+            [ones_where((column == start + width * j + (inner >> 1)) & (inner < kept), 0.5)
+             for j in range(4)], axis=0)
+
+    def halved(ref, x, start, count):
+        sums = None
+        for plane in (x, x + 1):
+            for odd in (0, 1):
+                term = ref[plane, pl.ds(start + odd, count, 2)]
+                sums = term if sums is None else sums + term
+        return sums
+
+    to_one = packing(32, bz, 0)
+
+    def pack_one(ref, first, start, out):
+        quads = []
         for q in range(half_x // 4):
-            sums = jnp.concatenate(
-                [plane(2 * (4 * q + j)) + plane(2 * (4 * q + j) + 1) for j in range(4)], axis=1)
-            out[q] = mm_left(rows_one, mm(sums, to_one))
-
-    pad_plane = jnp.zeros((by, 128 - bz), F32)
-    pack_one(lambda x: jnp.concatenate([a_ref[x], pad_plane], axis=1), own_a)
+            planes = [halved(ref, first + 2 * (4 * q + j), start, half_y) for j in range(4)]
+            if planes[0].shape[1] < 128:
+                pad = jnp.zeros((half_y, 128 - planes[0].shape[1]), F32)
+                planes = [jnp.concatenate([plane, pad], axis=1) for plane in planes]
+            quads.append(jnp.concatenate(planes, axis=1))
+        packed = mm(jnp.concatenate(quads, axis=0), to_one)
+        for q in range(half_x // 4):
+            out[q] = packed[q * half_y : (q + 1) * half_y]
+
+    pack_one(a_ref, 0, 0, own_a)
 
     offsets_x = (0,) if gx == 1 else ((0, 2) if gx == 2 else (-1, 0, 1))
 
@@ -252,9 +309,9 @@
 
     bricks(own_a, near_a, a_send, a_recv, "start")
 
-    to_two = ones_where((column == group * 16 + inner // 2) & (inner < half_z), 0.5)
-    to_two_a = ones_where((column == 64 + group * 16 + inner // 2) & (inner < half_z), 0.5)
-    rows_two = ones_where(iota((half_y // 2, half_y), 1) // 2 == iota((half_y // 2, half_y), 0))
+    to_two = packing(16, half_z, 0)
+    to_two_a = packing(16, half_z, 64)
+    rows_two = ones_where((iota((half_y // 2, half_y), 1) >> 1) == iota((half_y // 2, half_y), 0))
     lane = iota((8, 128), 1)
 
     def brick_plane(own, x):
@@ -320,7 +377,7 @@
     z_at = me_z * half_z + zoff
     mask_one = jnp.where(
         (row >= 0) & (row < gy * half_y) & (z_at >= 0) & (z_at < gz * half_z) & (zoff < 64), 1.0, 0.0)
-    lane_group = lane // 32
+    lane_group = lane >> 5
 
     def unpack_one(near, own, dst):
         near[(at_one // half_x) * 9 + 4] = own[...]
@@ -343,6 +400,13 @@
     bricks(own_a, near_a, a_send, a_recv, "recv")
     unpack_one(near_a, own_a, mid.diag)
 
+    def plane_ok(start, total):
+        if small_x:
+            return None
+        return lambda x: jnp.where((start + x >= 0) & (start + x < total), 1.0, 0.0)
+
+    mid.scale(lambda x: mid.diag[x], mask_one, plane_ok(me_x * half_x - half_x, gx * half_x))
+
     zoff0 = iota((by + 16, 128), 1)
     zoff0 = jnp.where(zoff0 < 96, zoff0, zoff0 - 128)
     row0 = me_y * by - 8 + iota((by + 16, 128), 0)
@@ -351,29 +415,23 @@
         (row0 >= 0) & (row0 < gy * by) & (z0 >= 0) & (z0 < gz * bz)
         & (zoff0 < bz + 8) & (zoff0 >= -8), 1.0, 0.0)
 
-    def plane_ok(start, total):
-        if small_x:
-            return None
-        return lambda x: jnp.where((start + x >= 0) & (start + x < total), 1.0, 0.0)
-
     for ox, oy in faces():
         copy, there = face_copy(ox, oy, True)
         guarded(there, copy.wait_recv)
-    fine.init(lambda x: window[0, x], lambda x: window[1, x], mask_zero,
-              plane_ok(me_x * bx - HX, gx * bx))
-    fine.down()
-
-    pack_one(lambda x: fine.r[at_x + x, 8 : 8 + by], own_f)
+    fine.scale(lambda x: window[1, x], mask_zero, plane_ok(me_x * bx - HX, gx * bx))
+    fine.init(lambda x: window[0, x])
+    fine.down(3)
+
+    pack_one(fine.r, at_x, 8, own_f)
     bricks(own_f, near_f, f_send, f_recv, "start")
+    fine.total(0, True)
     bricks(own_f, near_f, f_send, f_recv, "recv")
     unpack_one(near_f, own_f, mid.r)
-    mid.init(lambda x: mid.r[x], lambda x: mid.diag[x], mask_one,
-             plane_ok(me_x * half_x - half_x, gx * half_x))
-    mid.down()
-
-    sums = jnp.concatenate(
-        [mid.r[at_one + 2 * i, 8:16] + mid.r[at_one + 2 * i + 1, 8:16] for i in range(4)], axis=1)
-    share = mm_left(rows_two, mm(sums, to_two)) + share_a
+    mid.init(lambda x: mid.r[x])
+    mid.down(4)
+
+    sums = jnp.concatenate([halved(mid.r, at_one + 2 * i, 8, half_y // 2) for i in range(4)], axis=1)
+    share = mm(sums, to_two) + share_a
     pack[...] = share
     gathered[flat_me] = share
 
@@ -384,12 +442,13 @@
         return carry
 
     lax.fori_loop(1, devices, spread, 0)
+    mid.total(2, True)
     everything = pltpu.make_async_remote_copy(
         src_ref=gathered.at[0 : devices - 1], dst_ref=gathered.at[0 : devices - 1],
         send_sem=g_send, recv_sem=g_recv, device_id=place(1), device_id_type=MESH)
     everything.wait_recv()
 
-    lane16 = lane // 16
+    lane16 = lane >> 4
 
     def unpack_two(sx, carry):
         for pair in range(gy // 2):
@@ -417,80 +476,102 @@
         shape = (level.rows, level.lanes)
         return jnp.where((iota(shape, 0) < rows) & (iota(shape, 1) < lanes), 1.0, 0.0)
 
-    def matrices(above, below):
-        shape = (above.lanes, below.lanes)
-        narrow = ones_where(iota(shape, 0) // 2 == iota(shape, 1), 0.5)
-        shape = (below.rows, above.rows)
-        return narrow, ones_where(iota(shape, 1) // 2 == iota(shape, 0))
-
-    def restrict(src, dst, narrow, short):
-        for i in range(dst.shape[0]):
-            dst[i] = mm_left(short, mm(src[2 * i] + src[2 * i + 1], narrow))
-
-    def prolong(values, dst, wide, tall):
-        for i in range(values.shape[0]):
-            spread_out = mm_left(tall, mm(values[i], wide))
-            dst[2 * i + 1, 8 : 8 + dst.shape[1] - 16] = spread_out
-            dst[2 * i + 2, 8 : 8 + dst.shape[1] - 16] = spread_out
-
-    def wide_tall(above, below):
+    def restrict(src, dst):
+        planes, lanes = dst.shape[0], src.shape[2]
+        shape = (lanes, dst.shape[2])
+        narrow = ones_where((iota(shape, 0) >> 1) == iota(shape, 1), 0.5)
+        sums = [src[2 * i] + src[2 * i + 1] for i in range(planes)]
+        out = mm(jnp.concatenate(sums, axis=0), narrow)
+        shape = (dst.shape[1], src.shape[1])
+        fold = ones_where((iota(shape, 1) >> 1) == iota(shape, 0))
+        size = src.shape[1]
+        beside_each_other = jnp.concatenate(
+            [out[i * size : (i + 1) * size] for i in range(planes)], axis=1)
+        out = mm_left(fold, beside_each_other)
+        for i in range(planes):
+            dst[i] = out[:, i * dst.shape[2] : (i + 1) * dst.shape[2]]
+
+    def prolong(values, rows, wide, dst):
+        out = mm(jnp.concatenate(values, axis=0), wide)
+        if dst.shape[2] != 128:
+            shape = (2 * rows, rows)
+            tall = ones_where((iota(shape, 0) >> 1) == iota(shape, 1))
+            for i in range(len(values)):
+                doubled = mm_left(tall, out[i * rows : (i + 1) * rows])
+                for plane in (2 * i + 1, 2 * i + 2):
+                    dst[plane, 8 : 8 + 2 * rows] = doubled
+            return
+        for i in range(len(values)):
+            for plane in (2 * i + 1, 2 * i + 2):
+                for odd in (0, 1):
+                    dst[plane, pl.ds(8 + odd, rows, 2)] = out[i * rows : (i + 1) * rows]
+
+    def widening(above, below):
         shape = (below.lanes, above.lanes)
-        wide = ones_where(iota(shape, 1) // 2 == iota(shape, 0))
-        shape = (above.rows, below.rows)
-        return wide, ones_where(iota(shape, 0) // 2 == iota(shape, 1))
+        return ones_where((iota(shape, 1) >> 1) == iota(shape, 0))
 
     y2, z2 = gy * half_y // 2, gz * half_z // 2
-    narrow2, short2 = matrices(two, three)
-    narrow3, short3 = matrices(three, four)
-    restrict(whole_a, a3, narrow2, short2)
-    restrict(a3, a4, narrow3, short3)
-    two.init(lambda x: whole_f[x], lambda x: whole_a[x], whole_mask(two, y2, z2), unroll=4)
-    two.down(unroll=4)
-    restrict(two.r, f3, narrow2, short2)
-    three.init(lambda x: f3[x], lambda x: a3[x], whole_mask(three, y2 // 2, z2 // 2), unroll=4)
-    three.down(unroll=4)
-    restrict(three.r, f4, narrow3, short3)
-    four.init(lambda x: f4[x], lambda x: a4[x], whole_mask(four, y2 // 4, z2 // 4))
-    four.down(False)
-    prolong(four.v, three.d0, *wide_tall(three, four))
-    three.up(unroll=4)
-    prolong(three.v, two.d0, *wide_tall(two, three))
-    two.up(unroll=4)
+    restrict(whole_a, a3)
+    restrict(a3, a4)
+    two.scale(lambda x: whole_a[x], whole_mask(two, y2, z2))
+    three.scale(lambda x: a3[x], whole_mask(three, y2 // 2, z2 // 2))
+    four.scale(lambda x: a4[x], whole_mask(four, y2 // 4, z2 // 4))
+    two.init(lambda x: whole_f[x])
+    two.down()
+    two.total(0, True)
+    restrict(two.r, f3)
+    three.init(lambda x: f3[x])
+    three.down()
+    three.total(0, True)
+    restrict(three.r, f4)
+    four.init(lambda x: f4[x])
+    four.down(0, False)
+    four.total(0, True)
+    prolong([four.v[i, 0 : three.rows // 2] for i in range(four.planes)], three.rows // 2,
+            widening(three, four), three.d0)
+    three.up()
+    three.total_last()
+    prolong([three.v[i] for i in range(three.planes)], three.rows, widening(two, three), two.d0)
+    two.up()
+    two.total_last()
 
     shape = (two.lanes, 128)
     zoff1 = iota(shape, 1)
     zoff1 = jnp.where(zoff1 < 96, zoff1, zoff1 - 128)
-    coarse_z = (me_z * half_z + zoff1 + 2 * z2) // 2 - z2
+    coarse_z = (me_z * half_z + zoff1) >> 1
     wide = ones_where((iota(shape, 0) == coarse_z) & (iota(shape, 0) < z2))
     shape = (mid.rows, two.rows)
-    coarse_y = (me_y * half_y - half_y + iota(shape, 0) + 2 * y2) // 2 - y2
+    coarse_y = (me_y * half_y - half_y + iota(shape, 0)) >> 1
     tall = ones_where(iota(shape, 1) == coarse_y)
-    pairs = mid.planes // 2
-    for i in range(pairs):
+    values = []
+    for i in range(mid.planes // 2):
         if small_x:
-            values = two.v[i]
+            values.append(two.v[i])
         else:
             at = me_x * (half_x // 2) - half_x // 2 + i
             inside = (at >= 0) & (at < two.planes)
-            values = two.v[jnp.clip(at, 0, two.planes - 1)] * jnp.where(inside, 1.0, 0.0)
-        spread_out = mm_left(tall, mm(values, wide))
+            values.append(two.v[jnp.clip(at, 0, two.planes - 1)] * jnp.where(inside, 1.0, 0.0))
+    out = mm(jnp.concatenate(values, axis=0), wide)
+    size = two.rows
+    out = mm_left(tall, jnp.concatenate(
+        [out[i * size : (i + 1) * size] for i in range(len(values))], axis=1))
+    for i in range(len(values)):
+        spread_out = out[:, 128 * i : 128 * i + 128]
         mid.d0[2 * i + 1, 8 : 8 + mid.rows] = spread_out
         mid.d0[2 * i + 2, 8 : 8 + mid.rows] = spread_out
-    mid.up()
+    mid.up(2)
+    mid.total_last(2)
 
     shape = (128, 128)
     lane0 = iota(shape, 1)
-    from_lane = jnp.where(lane0 < 96, lane0 // 2, 64 + lane0 // 2)
+    from_lane = jnp.where(lane0 < 96, lane0 >> 1, 64 + (lane0 >> 1))
     wide = ones_where((iota(shape, 0) == from_lane) & ((lane0 < bz + 8) | (lane0 >= 120)))
-    shape = (fine.rows, mid.rows)
-    tall = ones_where(iota(shape, 1) == iota(shape, 0) // 2 + 4)
     at = (bx // 2 - HX // 2) * me_x if small_x else bx // 2 - HX // 2
-    for i in range(fine.planes // 2):
-        spread_out = mm_left(tall, mm(mid.v[at + i], wide))
-        fine.d0[2 * i + 1, 8 : 8 + fine.rows] = spread_out
-        fine.d0[2 * i + 2, 8 : 8 + fine.rows] = spread_out
-    fine.up(True)
-    p_ref[...] = fine.v[pl.ds(at_x, bx), 8 : 8 + by, 0:bz]
+    rows = fine.rows // 2
+    prolong([mid.v[at + i, 4 : 4 + rows] for i in range(fine.planes // 2)], rows, wide, fine.d0)
+    fine.up(1, True)
+    p_ref[...] = (fine.v[pl.ds(at_x, bx), 8 : 8 + by]
+                  + fine.d0[pl.ds(at_x + 1, bx), 16 : 16 + by])[:, :, 0:bz]
     e_ref[...] = fine.r[pl.ds(at_x, bx), 8 : 8 + by, 0:bz]
 
     pl.when(has_high)(lambda: z_copy(1).wait_send())
@@ -515,7 +596,7 @@
     def level(planes, rows, lanes):
         plain = pltpu.VMEM((planes, rows, lanes), F32)
         padded = pltpu.VMEM((planes + 2, rows + 16, lanes), F32)
-        return [plain] * 4 + [padded] * 2
+        return [plain] * 4 + [padded] * 3
 
     two = (gx * bx // 4, gy * by // 4, lanes_for(gz * bz // 4))
     three = (gx * bx // 8, gy * by // 8, lanes_for(gz * bz // 8))

time: 48.7 us -> 33.8 us (0.69)
  Pallas kernels: 45.7 us -> 30.8 us
    pallas_call x1, Pallas kernels: 45.7 us -> 30.8 us  [shards(): pl.pallas_call(functools.partial(kernel, counts), out_shape=(out, out), i...]
where the time goes in v2:
time: 33.8 us; the launch traced here: 33.7 us
  Pallas kernels  30.8 us (91%)
  local copies, waits for them, and re-layouts  2.26 us (7%)
  between operations  0.65 us (2%)
    pallas_call x1, Pallas kernels, shards(): pl.pallas_call(functools.partial(kernel, counts), out_shape=(out, out), i...  30.8 us
    unnamed x4, local copies, waits for them, and re-layouts  2.26 us

profile of v2, /device:TPU:0, one launch (start us, length us, event | category | flops | bytes accessed | tf_op | source)
XLA Modules:
  0.0 33.7 jit_solution(758008429447352596)
XLA Ops:
  0.6 30.8 %shard_map.41 = (f32[16,16,64]{2,1,0:T(8,128)}, f32[16,16,64]{2,1,0:T(8,128)}) custom-call(f32[16,16,64]{2,1,0:T(8,128)} %f_ref.1, f32[16,16,64]{2,1,0:T(8,128)} %a_ref.1), custom_call_target="tpu_custom_call" | custom-call | tf_op jit(solution)/shard_map/pallas_call | solution.py:632
  31.4 0.0 copy-start
  31.4 1.6 %copy.6 = f32[16,16,64]{2,1,0:T(8,128)} copy(f32[16,16,64]{2,1,0:T(8,128)} %get-tuple-element.4) | data formatting | bytes 131072
  33.0 0.0 copy-done
  33.0 0.7 %copy.7 = f32[16,16,64]{2,1,0:T(8,128)} copy(f32[16,16,64]{2,1,0:T(8,128)S(1)} %copy-done) | data formatting | bytes 131072
Async XLA Ops:
  31.4 1.6 %copy-start = (f32[16,16,64]{2,1,0:T(8,128)S(1)}, f32[16,16,64]{2,1,0:T(8,128)}, u32[]{:S(2)}) copy-start(f32[16,16,64]{2,1,0:T(8,128)} %get-tuple-element.5) | copy-start | bytes 196612

commit v3 on v2

--- a/solution.py
+++ b/solution.py
@@ -167,11 +167,12 @@
 
 
 def kernel(counts, f_ref, a_ref, p_ref, e_ref, turned, window, near_a, near_f, own_a, own_f,
-           pack, gathered, whole_f, whole_a, f3, a3, f4, a4, *rest):
+           pack, gathered, pack_a, gathered_a, whole_f, whole_a, f3, a3, f4, a4, *rest):
     gx, gy, gz = counts
     bx, by, bz = f_ref.shape
     devices = gx * gy * gz
-    z_send, z_recv, w_send, w_recv, a_send, a_recv, f_send, f_recv, g_send, g_recv = rest[35:]
+    z_send, z_recv, w_send, w_recv, a_send, a_recv, f_send, f_recv, g_send, g_recv, h_send, h_recv = (
+        rest[35:])
     me_x = lax.axis_index("gx")
     me_y = lax.axis_index("gy")
     me_z = lax.axis_index("gz")
@@ -185,32 +186,34 @@
     half_x, half_y, half_z = bx // 2, by // 2, bz // 2
 
     turned[...] = jnp.zeros_like(turned)
+    for ref in (near_a, near_f):
+        ref[...] = jnp.zeros_like(ref)
+
+    def clear_window(x, carry):
+        window[0, x] = jnp.zeros(window.shape[2:], F32)
+        window[1, x] = jnp.zeros(window.shape[2:], F32)
+        return carry
+
+    lax.fori_loop(0, window.shape[1], clear_window, 0)
+
+    barrier = pltpu.get_barrier_semaphore()
+    flat_me = (me_x * gy + me_y) * gz + me_z
+
+    def place(k):
+        other = lax.rem(flat_me + k, devices)
+        return (lax.div(other, gy * gz), lax.rem(lax.div(other, gz), gy), lax.rem(other, gz))
+
+    def greet(k, carry):
+        pl.semaphore_signal(barrier, inc=1, device_id=place(k), device_id_type=MESH)
+        return carry
+
+    lax.fori_loop(1, devices, greet, 0)
     padding = jnp.zeros((bx * by, 128 - bz), F32)
     for k, ref in enumerate((f_ref, a_ref)):
         flat = jnp.concatenate([ref[...].reshape(bx * by, bz), padding], axis=1)
         turned[0:bz, k * bx * by : (k + 1) * bx * by] = flat.T[0:bz]
-    for ref in (near_a, near_f, whole_f, whole_a, f4, a4):
+    for ref in (whole_f, whole_a, f4, a4):
         ref[...] = jnp.zeros_like(ref)
-
-    def clear_window(x, carry):
-        window[0, x] = jnp.zeros(window.shape[2:], F32)
-        window[1, x] = jnp.zeros(window.shape[2:], F32)
-        return carry
-
-    lax.fori_loop(0, window.shape[1], clear_window, 0)
-
-    barrier = pltpu.get_barrier_semaphore()
-    flat_me = (me_x * gy + me_y) * gz + me_z
-
-    def place(k):
-        other = lax.rem(flat_me + k, devices)
-        return (lax.div(other, gy * gz), lax.rem(lax.div(other, gz), gy), lax.rem(other, gz))
-
-    def greet(k, carry):
-        pl.semaphore_signal(barrier, inc=1, device_id=place(k), device_id_type=MESH)
-        return carry
-
-    lax.fori_loop(1, devices, greet, 0)
     pl.semaphore_wait(barrier, devices - 1)
 
     def z_copy(way):
@@ -310,7 +313,6 @@
     bricks(own_a, near_a, a_send, a_recv, "start")
 
     to_two = packing(16, half_z, 0)
-    to_two_a = packing(16, half_z, 64)
     rows_two = ones_where((iota((half_y // 2, half_y), 1) >> 1) == iota((half_y // 2, half_y), 0))
     lane = iota((8, 128), 1)
 
@@ -322,7 +324,24 @@
 
     sums = jnp.concatenate(
         [brick_plane(own_a, 2 * i) + brick_plane(own_a, 2 * i + 1) for i in range(4)], axis=1)
-    share_a = mm_left(rows_two, mm(sums, to_two_a))
+    share_a = mm_left(rows_two, mm(sums, to_two))
+    pack_a[...] = share_a
+    gathered_a[flat_me] = share_a
+
+    def spread(src, dst, send, recv):
+        def one(k, carry):
+            pltpu.make_async_remote_copy(
+                src_ref=src, dst_ref=dst.at[flat_me], send_sem=send, recv_sem=recv,
+                device_id=place(k), device_id_type=MESH).start()
+            return carry
+
+        lax.fori_loop(1, devices, one, 0)
+        return pltpu.make_async_remote_copy(
+            src_ref=dst.at[0 : devices - 1], dst_ref=dst.at[0 : devices - 1],
+            send_sem=send, recv_sem=recv, device_id=place(1), device_id_type=MESH)
+
+
+    everything_a = spread(pack_a, gathered_a, h_send, h_recv)
 
     for level in (fine, mid, two, three, four):
         level.clear()
@@ -407,70 +426,28 @@
 
     mid.scale(lambda x: mid.diag[x], mask_one, plane_ok(me_x * half_x - half_x, gx * half_x))
 
-    zoff0 = iota((by + 16, 128), 1)
-    zoff0 = jnp.where(zoff0 < 96, zoff0, zoff0 - 128)
-    row0 = me_y * by - 8 + iota((by + 16, 128), 0)
-    z0 = me_z * bz + zoff0
-    mask_zero = jnp.where(
-        (row0 >= 0) & (row0 < gy * by) & (z0 >= 0) & (z0 < gz * bz)
-        & (zoff0 < bz + 8) & (zoff0 >= -8), 1.0, 0.0)
-
-    for ox, oy in faces():
-        copy, there = face_copy(ox, oy, True)
-        guarded(there, copy.wait_recv)
-    fine.scale(lambda x: window[1, x], mask_zero, plane_ok(me_x * bx - HX, gx * bx))
-    fine.init(lambda x: window[0, x])
-    fine.down(3)
-
-    pack_one(fine.r, at_x, 8, own_f)
-    bricks(own_f, near_f, f_send, f_recv, "start")
-    fine.total(0, True)
-    bricks(own_f, near_f, f_send, f_recv, "recv")
-    unpack_one(near_f, own_f, mid.r)
-    mid.init(lambda x: mid.r[x])
-    mid.down(4)
-
-    sums = jnp.concatenate([halved(mid.r, at_one + 2 * i, 8, half_y // 2) for i in range(4)], axis=1)
-    share = mm(sums, to_two) + share_a
-    pack[...] = share
-    gathered[flat_me] = share
-
-    def spread(k, carry):
-        pltpu.make_async_remote_copy(
-            src_ref=pack, dst_ref=gathered.at[flat_me], send_sem=g_send, recv_sem=g_recv,
-            device_id=place(k), device_id_type=MESH).start()
-        return carry
-
-    lax.fori_loop(1, devices, spread, 0)
-    mid.total(2, True)
-    everything = pltpu.make_async_remote_copy(
-        src_ref=gathered.at[0 : devices - 1], dst_ref=gathered.at[0 : devices - 1],
-        send_sem=g_send, recv_sem=g_recv, device_id=place(1), device_id_type=MESH)
-    everything.wait_recv()
-
     lane16 = lane >> 4
 
-    def unpack_two(sx, carry):
-        for pair in range(gy // 2):
-            blocks = []
-            for sz in range(gz):
-                first = (sx * gy + 2 * pair) * gz + sz
-                both = jnp.concatenate([gathered[first], gathered[first + gz]], axis=0)
-                shift = 16 * (sz % 8)
-                blocks.append(pltpu.roll(both, shift, 1) if shift else both)
-            for k, dst in enumerate((whole_f, whole_a)):
+    def unpack_two(blocks_in, dst):
+        def one(sx, carry):
+            for pair in range(gy // 2):
+                blocks = []
+                for sz in range(gz):
+                    first = (sx * gy + 2 * pair) * gz + sz
+                    both = jnp.concatenate([blocks_in[first], blocks_in[first + gz]], axis=0)
+                    shift = 16 * (sz % 8)
+                    blocks.append(pltpu.roll(both, shift, 1) if shift else both)
                 for i in range(4):
                     for tile in range((gz + 7) // 8):
                         piece = jnp.zeros((8, 128), F32)
                         for sz in range(8 * tile, min(gz, 8 * tile + 8)):
-                            piece = jnp.where(lane16 == (4 * k + i + sz) % 8, blocks[sz], piece)
-                        shift = (128 - 16 * (4 * k + i)) % 128
-                        if shift:
-                            piece = pltpu.roll(piece, shift, 1)
+                            piece = jnp.where(lane16 == (i + sz) % 8, blocks[sz], piece)
+                        if i:
+                            piece = pltpu.roll(piece, 128 - 16 * i, 1)
                         dst[4 * sx + i, 8 * pair : 8 * pair + 8, 128 * tile : 128 * tile + 128] = piece
-        return carry
-
-    lax.fori_loop(0, gx, unpack_two, 0)
+            return carry
+
+        lax.fori_loop(0, gx, one, 0)
 
     def whole_mask(level, rows, lanes):
         shape = (level.rows, level.lanes)
@@ -510,12 +487,46 @@
         shape = (below.lanes, above.lanes)
         return ones_where((iota(shape, 1) >> 1) == iota(shape, 0))
 
+    zoff0 = iota((by + 16, 128), 1)
+    zoff0 = jnp.where(zoff0 < 96, zoff0, zoff0 - 128)
+    row0 = me_y * by - 8 + iota((by + 16, 128), 0)
+    z0 = me_z * bz + zoff0
+    mask_zero = jnp.where(
+        (row0 >= 0) & (row0 < gy * by) & (z0 >= 0) & (z0 < gz * bz)
+        & (zoff0 < bz + 8) & (zoff0 >= -8), 1.0, 0.0)
+
+    for ox, oy in faces():
+        copy, there = face_copy(ox, oy, True)
+        guarded(there, copy.wait_recv)
+    fine.scale(lambda x: window[1, x], mask_zero, plane_ok(me_x * bx - HX, gx * bx))
+    fine.init(lambda x: window[0, x])
+    fine.down(3)
+
+    pack_one(fine.r, at_x, 8, own_f)
+    bricks(own_f, near_f, f_send, f_recv, "start")
+    fine.total(0, True)
+    everything_a.wait_recv()
+    unpack_two(gathered_a, whole_a)
     y2, z2 = gy * half_y // 2, gz * half_z // 2
     restrict(whole_a, a3)
     restrict(a3, a4)
     two.scale(lambda x: whole_a[x], whole_mask(two, y2, z2))
     three.scale(lambda x: a3[x], whole_mask(three, y2 // 2, z2 // 2))
     four.scale(lambda x: a4[x], whole_mask(four, y2 // 4, z2 // 4))
+    bricks(own_f, near_f, f_send, f_recv, "recv")
+    unpack_one(near_f, own_f, mid.r)
+    mid.init(lambda x: mid.r[x])
+    mid.down(4)
+
+    sums = jnp.concatenate([halved(mid.r, at_one + 2 * i, 8, half_y // 2) for i in range(4)], axis=1)
+    share = mm(sums, to_two)
+    pack[...] = share
+    gathered[flat_me] = share
+
+    everything = spread(pack, gathered, g_send, g_recv)
+    mid.total(2, True)
+    everything.wait_recv()
+    unpack_two(gathered, whole_f)
     two.init(lambda x: whole_f[x])
     two.down()
     two.total(0, True)
@@ -582,6 +593,12 @@
         copy, there = face_copy(ox, oy, False)
         guarded(there, copy.wait_send)
     everything.wait_send()
+    everything_a.wait_send()
+
+
+def hand_on(p_ref, e_ref, pressure_ref, residual_ref):
+    pressure_ref[...] = p_ref[...]
+    residual_ref[...] = e_ref[...]
 
 
 def shards(counts, right_side, diagonal):
@@ -610,6 +627,8 @@
         pltpu.VMEM(near, F32),
         pltpu.VMEM(brick, F32),
         pltpu.VMEM(brick, F32),
+        pltpu.VMEM((by // 4, 128), F32),
+        pltpu.VMEM((gx * gy * gz, by // 4, 128), F32),
         pltpu.VMEM((by // 4, 128), F32),
         pltpu.VMEM((gx * gy * gz, by // 4, 128), F32),
         pltpu.VMEM(two, F32),
@@ -626,10 +645,10 @@
     scratch += [dma((2,)), dma((2,))]
     scratch += [dma((slots_x * 3,))] * 2
     scratch += [dma((slots_x * 9,))] * 4
-    scratch += [dma, dma]
+    scratch += [dma] * 4
     out = jax.ShapeDtypeStruct(right_side.shape, F32)
     vmem = pl.BlockSpec(memory_space=pltpu.VMEM)
-    return pl.pallas_call(
+    results = pl.pallas_call(
         functools.partial(kernel, counts),
         out_shape=(out, out),
         in_specs=[vmem, vmem],
@@ -639,6 +658,9 @@
             collective_id=0, has_side_effects=True, vmem_limit_bytes=56 * 1024 * 1024
         ),
     )(right_side, diagonal)
+    return pl.pallas_call(
+        hand_on, out_shape=(out, out), in_specs=[vmem, vmem], out_specs=(vmem, vmem)
+    )(*results)
 
 
 def solution(mesh):

time: 33.8 us -> 33.2 us (0.982)
  local copies, waits for them, and re-layouts: 2.26 us -> 0 us
  Pallas kernels: 30.8 us -> 32.4 us
    unnamed x4 -> x0, local copies, waits for them, and re-layouts: 2.26 us -> none
    pallas_call x0 -> x1, Pallas kernels: none -> 1.68 us  [shards(): pl.pallas_call(hand_on, out_shape=(out, out), in_specs=[vmem, vmem], out_...]
where the time goes in v3:
time: 33.2 us; the launch traced here: 33.1 us
  Pallas kernels  32.4 us (98%)
  between operations  0.64 us (2%)
    pallas_call x1, Pallas kernels, shards(): pl.pallas_call(functools.partial(kernel, counts), out_shape=(out, out), i...  30.8 us
    pallas_call x1, Pallas kernels, shards(): pl.pallas_call(hand_on, out_shape=(out, out), in_specs=[vmem, vmem], out_...  1.68 us

profile of v3, /device:TPU:0, one launch (start us, length us, event | category | flops | bytes accessed | tf_op | source)
XLA Modules:
  0.0 33.1 jit_solution(4093418831290154597)
XLA Ops:
  0.6 30.8 %shard_map.41 = (f32[16,16,64]{2,1,0:T(8,128)}, f32[16,16,64]{2,1,0:T(8,128)}) custom-call(f32[16,16,64]{2,1,0:T(8,128)} %f_ref.1, f32[16,16,64]{2,1,0:T(8,128)} %a_ref.1), custom_call_target="tpu_custom_call" | custom-call | tf_op jit(solution)/shard_map/pallas_call | solution.py:651
  31.4 1.7 %shard_map.42 = (f32[16,16,64]{2,1,0:T(8,128)}, f32[16,16,64]{2,1,0:T(8,128)}) custom-call(f32[16,16,64]{2,1,0:T(8,128)} %get-tuple-element.4.p_ref, f32[16,16,64]{2,1,0:T(8,128)} %get-tuple-element.5.e_ref), custom_call_target="tpu_custom_call" | custom-call | tf_op jit(solution)/shard_map/pallas_call | solution.py:661
